TPU v7x, 128 devices: a whole 4x4x4 slice. The times are simulated.
128 devices in a mesh: seq: 32 (over y, z, core), tp: 4 (over x).
Axes of the slice: x: 4, y: 4, z: 4, core: 2. Of those that a mesh axis runs over, the one named last changes fastest.
Arguments:
- tokens: bfloat16 [16384, 4096], P('seq', 'tp'), may hold values from -18 to 18
- weights: bfloat16 [3, 4096, 4096], P(None, 'seq', 'tp'), may hold values from -0.09375 to 0.09375
- gate_bias: float32 [3, 4096], P(None, 'tp'), may hold values from -16 to 8
- recurrent: float32 [3, 4096], P(None, 'tp'), may hold values from -0.5 to 0.5
- initial_state: float32 [4096], P('tp'), may hold values from -3 to 3
Outputs:
- states: float32 [16384, 4096], P('seq', 'tp')
All inputs are finite; a program needn't handle non-finite values.
Results may differ from a plain program's by a relative error of at most 0.0003.
Values may be sent and summed in bfloat16 or wider, within the bound.
A program may use at most 128 MiB of HBM per device.

v0:
```python
import jax
import jax.numpy as jnp
from jax import lax
from jax.sharding import PartitionSpec as P

ITERS = 2


def prefix(part, axis, combine, identity):
    place = lax.axis_index(axis)
    gathered = jax.tree.map(lambda a: lax.all_gather(a, axis), part)
    state = jax.tree.map(lambda a, e: jnp.zeros_like(a) + jnp.asarray(e, a.dtype), part, identity)

    def one(hop, state):
        return combine(
            state, jax.tree.map(lambda a: lax.dynamic_index_in_dim(a, hop, 0, False), gathered)
        )

    return lax.fori_loop(0, place, one, state)


def cell_terms(preact, previous, coeffs):
    update_gate = jax.nn.sigmoid(preact[0] + coeffs[0] * previous)
    reset_gate = jax.nn.sigmoid(preact[1] + coeffs[1] * previous)
    candidate = jnp.tanh(preact[2] + coeffs[2] * reset_gate * previous)
    stepped = (1.0 - update_gate) * previous + update_gate * candidate
    update_slope = update_gate * (1.0 - update_gate) * coeffs[0]
    reset_slope = reset_gate * (1.0 - reset_gate) * coeffs[1]
    candidate_slope = (
        (1.0 - candidate * candidate) * coeffs[2] * (reset_gate + previous * reset_slope)
    )
    jacobian = (
        1.0 - update_gate + (candidate - previous) * update_slope + update_gate * candidate_slope
    )
    return (stepped, jacobian)


def compose(earlier, later):
    return (earlier[0] * later[0], later[0] * earlier[1] + later[1])


def tiled_scan(jacobian, offset):
    token_rows, channels = jacobian.shape
    group_count = token_rows // 8
    group_rates = jacobian.reshape(group_count, 8, channels)
    group_terms = offset.reshape(group_count, 8, channels)
    run_rates = group_rates[:, 0]
    run_terms = group_terms[:, 0]
    rate_list = [run_rates]
    term_list = [run_terms]
    for inner in range(1, 8):
        run_terms = group_rates[:, inner] * run_terms + group_terms[:, inner]
        run_rates = group_rates[:, inner] * run_rates
        rate_list.append(run_rates)
        term_list.append(run_terms)
    inner_rates = jnp.stack(rate_list, axis=1)
    inner_terms = jnp.stack(term_list, axis=1)
    totals = lax.associative_scan(compose, (run_rates, run_terms), axis=0)
    leading_rates = jnp.concatenate([jnp.ones((1, channels), jnp.float32), totals[0][:-1]], axis=0)
    leading_terms = jnp.concatenate([jnp.zeros((1, channels), jnp.float32), totals[1][:-1]], axis=0)
    products = inner_rates * leading_rates[:, None, :]
    values = inner_rates * leading_terms[:, None, :] + inner_terms
    return (products.reshape(token_rows, channels), values.reshape(token_rows, channels))


def body(tokens, weights, gate_bias, recurrent, initial_state):
    features = lax.all_gather(tokens, "tp", axis=1, tiled=True)
    channels = weights.shape[2]
    token_rows = tokens.shape[0]
    preact = jnp.einsum(
        "tk,gkc->gtc",
        features,
        lax.all_gather(weights, "seq", axis=1, tiled=True),
        preferred_element_type=jnp.float32,
    )
    preact = preact + gate_bias[:, None, :]
    position = lax.axis_index("seq")
    carried = jnp.where(position == 0, initial_state, jnp.zeros_like(initial_state))
    state = jnp.zeros((token_rows, channels), jnp.float32)
    identity_pair = (jnp.ones((1, channels), jnp.float32), jnp.zeros((1, channels), jnp.float32))
    for iteration in range(ITERS):
        previous = jnp.concatenate([carried[None, :], state[:-1]], axis=0)
        stepped, jacobian = cell_terms(preact, previous, recurrent[:, None, :])
        offset = stepped - jacobian * previous
        products, values = tiled_scan(jacobian, offset)
        summary = (products[-1:], values[-1:])
        before = prefix(summary, "seq", compose, identity_pair)
        incoming = before[0][0] * initial_state + before[1][0]
        state = values + products * incoming[None, :]
        carried = incoming
    return state


def solution(mesh):
    return jax.shard_map(
        body,
        mesh=mesh,
        in_specs=(P("seq", "tp"), P(None, "seq", "tp"), P(None, "tp"), P(None, "tp"), P("tp")),
        out_specs=P("seq", "tp"),
        check_vma=False,
    )
```

profile of v0, /device:TPU:1, one launch (start us, length us, event | category | flops | bytes accessed | tf_op | source)
XLA Modules:
  0.0 359.5 jit_solution(1236457798445558951)
XLA Ops:
  6.5 0.7 all-gather.13.cloned.1.call-update
  7.3 0.7 all-gather.11.cloned.1.call-update
  8.0 0.8 fusion.73
  8.9 51.6 %all-gather.13.cloned.1.call-done = bf16[512,4096]{1,0:T(8,128)(2,1)} async-done(((bf16[512,1024]{1,0:T(8,128)(2,1)}), bf16[512,4096]{1,0:T(8,128)(2,1)}) %all-gather.13.cloned.1.call-update) | async-done | bytes 4194320 | tf_op jit(solution)/shard_map/all_gather | solution.py:67
  60.5 95.5 %all-gather.11.cloned.1.call-done = bf16[3,4096,1024]{2,1,0:T(8,128)(2,1)} async-done(((bf16[3,128,1024]{2,1,0:T(8,128)(2,1)}), bf16[3,4096,1024]{2,1,0:T(8,128)(2,1)}) %all-gather.11.cloned.1.call-update) | async-done | bytes 25165840 | tf_op jit(solution)/shard_map/all_gather | solution.py:73
  155.9 18.0 %add_bitcast_fusion = f32[3,512,1024]{2,1,0:T(8,128)S(1)} fusion(f32[3,1024]{1,0:T(4,128)} %param.11, bf16[3,4096,1024]{2,1,0:T(8,128)(2,1)} %all-gather.11.cloned.1.call-done, bf16[512,4096]{1,0:T(8,128)(2,1)} %all-gather.13.cloned.1.call-done), kind=kOutput, calls=%fused_computation.13 | convolution fusion | flops 12886474752 | bytes 35663872 | tf_op jit(solution)/shard_map/tk,gkc->gtc/dot_general | solution.py:70
  173.9 3.4 fusion.35
  177.3 2.5 slice_multiply_fusion.8
  179.9 0.7 slice.551
  181.4 11.9 %slice_add_fusion.8 = (f32[64,1,1024]{2,1,0:T(1,128)S(1)}, f32[64,1,1024]{2,1,0:T(1,128)}, f32[64,1,1024]{2,1,0:T(1,128)}, f32[64,1,1024]{2,1,0:T(1,128)}, f32[6...) fusion(f32[64,8,1024]{2,1,0:T(8,128)} %get-tuple-element.131, ...), kind=kLoop, calls=%fused_computation.82 | loop fusion | flops 917504 | bytes 6029312 | tf_op jit(solution)/shard_map/add | solution.py:52
  193.4 0.9 fusion.64
  196.6 0.7 concatenate.86
  197.4 0.7 concatenate.92
  198.2 4.7 %stack.8 = f32[64,8,1024]{2,1,0:T(8,128)} concatenate(f32[64,1,1024]{2,1,0:T(1,128)S(1)} %copy-done.6, f32[64,1,1024]{2,1,0:T(1,128)S(1)} %copy-done.5, f32[64,1,1024]{2,1,0:T(1,128)S(1)} %copy-done.4, f32[64,1,1024]{2,1,0:T(1,128)S(1)} %copy-done.3, f32[64,1,1024]{2,1,0:T(1,128)S(1)} %get-tuple-element.120, f32[64,1,1024]{2,1,0:T(1,128)S(1)} %get-tuple-element.119, ...), dimensions={1} | concatenate | bytes 4194304 | tf_op jit(solution)/shard_map/stack | solution.py:56
  203.0 6.3 %stack.9 = f32[64,8,1024]{2,1,0:T(8,128)} concatenate(f32[64,1,1024]{2,1,0:T(1,128)} %get-tuple-element.144, f32[64,1,1024]{2,1,0:T(1,128)} %get-tuple-element.130, f32[64,1,1024]{2,1,0:T(1,128)} %get-tuple-element.129, f32[64,1,1024]{2,1,0:T(1,128)S(1)} %copy-done.14, f32[64,1,1024]{2,1,0:T(1,128)S(1)} %copy-done.13, f32[64,1,1024]{2,1,0:T(1,128)S(1)} %copy-done.12, ...), dimensions={1} | concatenate | bytes 4194304 | tf_op jit(solution)/shard_map/stack | solution.py:57
  209.3 2.9 multiply_bitcast_fusion.1
  212.2 24.5 %all-gather.4 = f32[32,1,1024]{2,1,0:T(1,128)S(1)} all-gather(f32[1,1,1024]{2,1,0:T(1,128)S(1)} %slice_bitcast_fusion.6), channel_id=2, replica_groups=mesh['seq'=32,'tp'=4] {'seq'}, dimensions={0}, use_global_device_ids=true | all-gather | bytes 135168 | tf_op jit(solution)/shard_map/all_gather | solution.py:11
  236.7 22.4 %all-gather.5 = f32[32,1,1024]{2,1,0:T(1,128)S(1)} all-gather(f32[1,1,1024]{2,1,0:T(1,128)S(1)} %slice_bitcast_fusion.4), channel_id=3, replica_groups=mesh['seq'=32,'tp'=4] {'seq'}, dimensions={0}, use_global_device_ids=true | all-gather | bytes 135168 | tf_op jit(solution)/shard_map/all_gather | solution.py:11
  259.2 2.0 slice_add_fusion
  261.2 5.6 %fusion.11 = (f32[64,8,1024]{2,1,0:T(8,128)}, f32[64,8,1024]{2,1,0:T(8,128)S(1)}) fusion(f32[3,512,1024]{2,1,0:T(8,128)} %copy-done, f32[511,1024]{1,0:T(8,128)S(1)} %slice_add_fusion, f32[1,1024]{1,0:T(1,128)S(1)} %bitcast.175, f32[1024]{0:T(1024)S(1)} %bitcast.174, f32[1024]{0:T(1024)S(1)} %bitcast.170, f32[1024]{0:T(1024)S(1)} %bitcast.172), kind=kLoop, calls=%fused_computation.30 | loop fusion | flops 18874368 | bytes 12595200 | tf_op jit(solution)/shard_map/sub | solution.py:84
  266.8 2.5 slice_multiply_fusion.1
  269.4 0.7 slice.609
  270.9 11.9 %slice_add_fusion.1 = (f32[64,1,1024]{2,1,0:T(1,128)S(1)}, f32[64,1,1024]{2,1,0:T(1,128)}, f32[64,1,1024]{2,1,0:T(1,128)}, f32[64,1,1024]{2,1,0:T(1,128)}, f32[6...) fusion(f32[64,8,1024]{2,1,0:T(8,128)} %get-tuple-element.115, ...), kind=kLoop, calls=%fused_computation.75 | loop fusion | flops 917504 | bytes 6029312 | tf_op jit(solution)/shard_map/add | solution.py:52
  282.9 0.9 fusion.63
  286.1 0.7 concatenate.106
  287.0 0.7 concatenate.100
  287.7 4.7 %stack.10 = f32[64,8,1024]{2,1,0:T(8,128)} concatenate(f32[64,1,1024]{2,1,0:T(1,128)S(1)} %copy-done.10, f32[64,1,1024]{2,1,0:T(1,128)S(1)} %copy-done.9, f32[64,1,1024]{2,1,0:T(1,128)S(1)} %copy-done.8, f32[64,1,1024]{2,1,0:T(1,128)S(1)} %copy-done.7, f32[64,1,1024]{2,1,0:T(1,128)S(1)} %get-tuple-element.104, f32[64,1,1024]{2,1,0:T(1,128)S(1)} %get-tuple-element.103, ...), dimensions={1} | concatenate | bytes 4194304 | tf_op jit(solution)/shard_map/stack | solution.py:56
  292.5 6.3 %stack.11 = f32[64,8,1024]{2,1,0:T(8,128)} concatenate(f32[64,1,1024]{2,1,0:T(1,128)} %get-tuple-element.140, f32[64,1,1024]{2,1,0:T(1,128)} %get-tuple-element.114, f32[64,1,1024]{2,1,0:T(1,128)} %get-tuple-element.113, f32[64,1,1024]{2,1,0:T(1,128)S(1)} %copy-done.18, f32[64,1,1024]{2,1,0:T(1,128)S(1)} %copy-done.17, f32[64,1,1024]{2,1,0:T(1,128)S(1)} %copy-done.16, ...), dimensions={1} | concatenate | bytes 4194304 | tf_op jit(solution)/shard_map/stack | solution.py:57
  298.8 2.9 multiply_bitcast_fusion
  301.7 24.9 %all-gather.6 = f32[32,1,1024]{2,1,0:T(1,128)S(1)} all-gather(f32[1,1,1024]{2,1,0:T(1,128)S(1)} %slice_bitcast_fusion.1), channel_id=4, replica_groups=mesh['seq'=32,'tp'=4] {'seq'}, dimensions={0}, use_global_device_ids=true | all-gather | bytes 135168 | tf_op jit(solution)/shard_map/all_gather | solution.py:11
  326.6 22.6 %all-gather.7 = f32[32,1,1024]{2,1,0:T(1,128)S(1)} all-gather(f32[1,1,1024]{2,1,0:T(1,128)S(1)} %slice_bitcast_fusion), channel_id=5, replica_groups=mesh['seq'=32,'tp'=4] {'seq'}, dimensions={0}, use_global_device_ids=true | all-gather | bytes 135168 | tf_op jit(solution)/shard_map/all_gather | solution.py:11
  349.3 3.4 multiply_add_fusion
  (245 shorter events, 5.9 us)
Async XLA Ops:
  6.5 53.9 %all-gather.13.cloned.1.call-start = ((), (), s32[]{:S(2)}) async-start(), calls=%async_computation.1 | async-start | bytes 5242880 | tf_op jit(solution)/shard_map/all_gather | solution.py:67
  7.3 148.7 %all-gather.11.cloned.1.call-start = ((), (), s32[]{:S(2)}) async-start(), calls=%async_computation | async-start | bytes 25952256 | tf_op jit(solution)/shard_map/all_gather | solution.py:73
  173.9 3.4 copy-start
  195.4 0.9 copy-start.23
  196.4 1.7 copy-start.3
  196.5 1.7 copy-start.4
  196.5 1.7 copy-start.5
  196.5 1.7 copy-start.6
  198.2 4.7 %copy-start.11 = (f32[64,1,1024]{2,1,0:T(1,128)S(1)}, f32[64,1,1024]{2,1,0:T(1,128)}, u32[]{:S(2)}) copy-start(f32[64,1,1024]{2,1,0:T(1,128)} %get-tuple-element.125) | copy-start | bytes 786436
  198.2 4.7 %copy-start.12 = (f32[64,1,1024]{2,1,0:T(1,128)S(1)}, f32[64,1,1024]{2,1,0:T(1,128)}, u32[]{:S(2)}) copy-start(f32[64,1,1024]{2,1,0:T(1,128)} %get-tuple-element.126) | copy-start | bytes 786436
  198.2 4.7 %copy-start.13 = (f32[64,1,1024]{2,1,0:T(1,128)S(1)}, f32[64,1,1024]{2,1,0:T(1,128)}, u32[]{:S(2)}) copy-start(f32[64,1,1024]{2,1,0:T(1,128)} %get-tuple-element.127) | copy-start | bytes 786436
  198.2 4.7 %copy-start.14 = (f32[64,1,1024]{2,1,0:T(1,128)S(1)}, f32[64,1,1024]{2,1,0:T(1,128)}, u32[]{:S(2)}) copy-start(f32[64,1,1024]{2,1,0:T(1,128)} %get-tuple-element.128) | copy-start | bytes 786436
  202.9 6.3 %copy-start.19 = (f32[64,1024]{1,0:T(8,128)S(1)}, f32[64,1024]{1,0:T(8,128)}, u32[]{:S(2)}) copy-start(f32[64,1024]{1,0:T(8,128)} %concatenate.86) | copy-start | bytes 786436
  202.9 6.3 %copy-start.21 = (f32[64,1024]{1,0:T(8,128)S(1)}, f32[64,1024]{1,0:T(8,128)}, u32[]{:S(2)}) copy-start(f32[64,1024]{1,0:T(8,128)} %concatenate.92) | copy-start | bytes 786436
  209.3 49.9 %copy-start.25 = (f32[1024]{0:T(1024)S(1)}, f32[1024]{0:T(1024)}, u32[]{:S(2)}) copy-start(f32[1024]{0:T(1024)} %param.13) | copy-start | bytes 12292
  212.2 24.5 %copy-start.2 = (f32[512,1024]{1,0:T(8,128)}, f32[512,1024]{1,0:T(8,128)S(1)}, u32[]{:S(2)}) copy-start(f32[512,1024]{1,0:T(8,128)S(1)} %get-tuple-element.142) | copy-start | bytes 6291460
  284.9 0.9 copy-start.24
  286.0 1.7 copy-start.7
  286.0 1.7 copy-start.8
  286.0 1.7 copy-start.9
  286.0 1.7 copy-start.10
  287.7 4.7 %copy-start.15 = (f32[64,1,1024]{2,1,0:T(1,128)S(1)}, f32[64,1,1024]{2,1,0:T(1,128)}, u32[]{:S(2)}) copy-start(f32[64,1,1024]{2,1,0:T(1,128)} %get-tuple-element.109) | copy-start | bytes 786436
  287.7 4.7 %copy-start.16 = (f32[64,1,1024]{2,1,0:T(1,128)S(1)}, f32[64,1,1024]{2,1,0:T(1,128)}, u32[]{:S(2)}) copy-start(f32[64,1,1024]{2,1,0:T(1,128)} %get-tuple-element.110) | copy-start | bytes 786436
  287.7 4.7 %copy-start.17 = (f32[64,1,1024]{2,1,0:T(1,128)S(1)}, f32[64,1,1024]{2,1,0:T(1,128)}, u32[]{:S(2)}) copy-start(f32[64,1,1024]{2,1,0:T(1,128)} %get-tuple-element.111) | copy-start | bytes 786436
  287.7 4.7 %copy-start.18 = (f32[64,1,1024]{2,1,0:T(1,128)S(1)}, f32[64,1,1024]{2,1,0:T(1,128)}, u32[]{:S(2)}) copy-start(f32[64,1,1024]{2,1,0:T(1,128)} %get-tuple-element.112) | copy-start | bytes 786436
  292.4 6.3 %copy-start.20 = (f32[64,1024]{1,0:T(8,128)S(1)}, f32[64,1024]{1,0:T(8,128)}, u32[]{:S(2)}) copy-start(f32[64,1024]{1,0:T(8,128)} %concatenate.106) | copy-start | bytes 786436
  292.5 6.3 %copy-start.22 = (f32[64,1024]{1,0:T(8,128)S(1)}, f32[64,1024]{1,0:T(8,128)}, u32[]{:S(2)}) copy-start(f32[64,1024]{1,0:T(8,128)} %concatenate.100) | copy-start | bytes 786436
  301.7 24.9 %copy-start.1 = (f32[512,1024]{1,0:T(8,128)}, f32[512,1024]{1,0:T(8,128)S(1)}, u32[]{:S(2)}) copy-start(f32[512,1024]{1,0:T(8,128)S(1)} %get-tuple-element.138) | copy-start | bytes 6291460
Sparse Core Ops, SparseCore 0:
  9.0 51.3 all-gather.12
  62.8 93.0 all-gather.10
where the time goes:
time: 361 us; the launch traced here: 360 us
  waiting for transfers between devices  148 us (41%)
  blocking collectives  94.4 us (26%)
  other arithmetic  52.1 us (14%)
  local copies, waits for them, and re-layouts  31.8 us (9%)
  matrix products  18 us (5%)
  between operations  14.8 us (4%)
    all_gather x1, waiting for transfers between devices, body(): lax.all_gather(weights, 'seq', axis=1, tiled=True)  95.5 us
    all_gather x4, blocking collectives, prefix(): gathered = jax.tree.map(lambda a: lax.all_gather(a, axis), part)  94.4 us
    all_gather x1, waiting for transfers between devices, body(): features = lax.all_gather(tokens, 'tp', axis=1, tiled=True)  51.6 us
    add x2, other arithmetic, tiled_scan(): run_terms = group_rates[:, inner] * run_terms + group_terms[:, inner]  23.8 us
    dot_general x1, matrix products, body(): jnp.einsum('tk,gkc->gtc', features, lax.all_gather(weights, 'seq', axis=1...  18 us
    another operation x2, local copies, waits for them, and re-layouts, tiled_scan(): inner_terms = jnp.stack(term_list, axis=1)  12.6 us
    another operation x2, local copies, waits for them, and re-layouts, tiled_scan(): inner_rates = jnp.stack(rate_list, axis=1)  9.39 us
  transfers between devices with their start and end apart: 2, of which 2 were waited for; matrix products, arithmetic and copies ran while one was open for 0% of the time, Pallas kernels for 0%

commit v1 on v0

v1 whole, which is shorter than its diff:
```python
import functools

import jax
import jax.numpy as jnp
from jax import lax
from jax.experimental import pallas as pl
from jax.experimental.pallas import tpu as pltpu
from jax.sharding import PartitionSpec as P

MESH = pl.DeviceIdType.MESH
RING = 4
CHIPS = RING * RING
CH = 128
CHUNKS = 4
TOK = 512
ROWS = 2 * TOK
FEAT = 1024
DEPTH = CHIPS * 256
SEGS = 8
SEG = ROWS // SEGS


def sigmoid(v):
    return jax.nn.sigmoid(v)


def cell(pre, p, coef):
    u = sigmoid(pre[0] + coef[0] * p)
    r = sigmoid(pre[1] + coef[1] * p)
    c = jnp.tanh(pre[2] + coef[2] * r * p)
    keep = 1.0 - u
    slope = c - p
    jac = (
        keep
        + slope * (u * keep * coef[0])
        + u * ((1.0 - c * c) * coef[2]) * (r + p * (r * (1.0 - r) * coef[1]))
    )
    stepped = keep * p + u * c
    return jac, stepped - jac * p


def cell_at_zero(pre, coef):
    u = sigmoid(pre[0])
    r = sigmoid(pre[1])
    c = jnp.tanh(pre[2])
    keep = 1.0 - u
    jac = keep + c * (u * keep * coef[0]) + u * ((1.0 - c * c) * coef[2]) * r
    return jac, u * c


def kernel(
    tok_hbm, w_hbm, bias, rec, init, out_hbm,
    X, W, PRE, AB1, AB2, OUTB, SEGT, SUM, SLOT,
    local_sem, sib_s, sib_r, p1_s, p1_r, p2_s, p2_r, t_s, t_r, ts_s, ts_r,
    ex_s, ex_r, o_l, o_s, o_r,
):
    seq, x = lax.axis_index("seq"), lax.axis_index("tp")
    c = lax.rem(seq, 2)
    q = seq // 2
    y, z = q // RING, lax.rem(q, RING)
    p = (1 - c) * y + c * z
    s = (1 - c) * z + c * y

    def block(pp, ss):
        return lax.rem(pp, RING) * (4 - 3 * c) + lax.rem(ss, RING) * (1 + 3 * c)

    def peer(qq):
        return (qq * 2 + c, x)

    right, left = peer(block(p + 1, s)), peer(block(p + 3, s))
    up, down = peer(block(p, s + 1)), peer(block(p, s + 3))
    xr, xl = (seq, lax.rem(x + 1, RING)), (seq, lax.rem(x + 3, RING))
    sib = (q * 2 + 1 - c, x)

    barrier = pltpu.get_barrier_semaphore()

    def greet(e, _):
        pl.semaphore_signal(
            barrier, inc=1, device_id=peer(lax.rem(q + e, CHIPS)), device_id_type=MESH
        )
        return 0

    lax.fori_loop(1, CHIPS, greet, 0)
    for d in (xr, xl, sib):
        pl.semaphore_signal(barrier, inc=1, device_id=d, device_id_type=MESH)
    pl.semaphore_wait(barrier, CHIPS + 2)

    def rcopy(src, dst, ss, rs, dev):
        return pltpu.make_async_remote_copy(
            src_ref=src, dst_ref=dst, send_sem=ss, recv_sem=rs, device_id=dev, device_id_type=MESH
        )

    sends = []

    def send(ref, ss, rs, dev, dst=None):
        cp = rcopy(ref, ref if dst is None else dst, ss, rs, dev)
        cp.start()
        sends.append((ref if dst is None else dst, ss))

    def arrived(ref, sem):
        pltpu.make_async_copy(ref, ref, sem).wait()

    def wrows(k, blk, half=None):
        start = blk * 256
        if half is None:
            return W.at[k, pl.ds(pl.multiple_of(start, 256), 256)]
        return W.at[k, pl.ds(pl.multiple_of(start + half * 128, 128), 128)]

    def chan(core, k):
        return pl.ds(pl.multiple_of(core * (CH * CHUNKS) + k * CH, CH), CH)

    for k in range(CHUNKS):
        for g in range(3):
            lanes = pl.ds(g * CH, CH)
            mine = pl.ds(pl.multiple_of(q * 256 + c * 128, 128), 128)
            pltpu.make_async_copy(
                w_hbm.at[g, :, chan(c, k)], W.at[k, mine, lanes], local_sem.at[k]
            ).start()
            rcopy(
                w_hbm.at[g, :, chan(1 - c, k)], W.at[k, mine, lanes], sib_s.at[k], sib_r.at[k], sib
            ).start()

    def trows(core, half=None):
        if half is None:
            return pl.ds(pl.multiple_of(core * TOK, TOK), TOK)
        return pl.ds(pl.multiple_of(core * TOK + half * 256, 256), 256)

    def tcols(xx):
        return pl.ds(pl.multiple_of(lax.rem(xx, RING) * FEAT, FEAT), FEAT)

    own_tok = pltpu.make_async_copy(tok_hbm, X.at[trows(c), tcols(x)], local_sem.at[CHUNKS])
    own_tok.start()

    for k in range(CHUNKS):
        own_half = wrows(k, q, c)
        arrived(own_half, local_sem.at[k])
        arrived(wrows(k, q, 1 - c), sib_r.at[k])
        piece = wrows(k, q)
        send(piece, p1_s.at[k, 0], p1_r.at[k, 0], right)
        send(piece, p1_s.at[k, 1], p1_r.at[k, 1], left)
    own_tok.wait()
    own_piece = X.at[trows(c), tcols(x)]
    send(own_piece, t_s.at[0], t_r.at[0], xr)
    send(own_piece, t_s.at[1], t_r.at[1], xl)
    send(own_piece, ts_s.at[0], ts_r.at[0], sib)

    def send2(k, i):
        piece = wrows(k, block(p + i, s))
        send(piece, p2_s.at[k, i, 0], p2_r.at[k, i, 0], up)
        send(piece, p2_s.at[k, i, 1], p2_r.at[k, i, 1], down)

    send2(0, 0)
    for k in range(CHUNKS):
        arrived(wrows(k, block(p + 3, s)), p1_r.at[k, 0])
        send(wrows(k, block(p + 3, s), 0), p1_s.at[k, 2], p1_r.at[k, 2], right)
        arrived(wrows(k, block(p + 1, s)), p1_r.at[k, 1])
        send(wrows(k, block(p + 1, s), 1), p1_s.at[k, 3], p1_r.at[k, 3], left)
        if k == 0:
            send2(0, 3)
            send2(0, 1)

    def row_of(ref, g, k):
        return ref[pl.ds(g, 1), chan(c, k)]

    def matmul(k):
        par = k % 2

        def tile(m, _):
            rows = pl.ds(pl.multiple_of(m * 256, 256), 256)
            acc = jnp.dot(X[rows, :], W[k], preferred_element_type=jnp.float32)
            for g in range(3):
                v = acc[:, g * CH : (g + 1) * CH] + row_of(bias, g, k)
                for h in range(2):
                    PRE[par, g, pl.ds(m * 2 + h, SEG, stride=SEGS), :] = v[h * SEG : (h + 1) * SEG]
            return 0

        lax.fori_loop(0, ROWS // 256, tile, 0)

    def vreg(j):
        return pl.ds(pl.multiple_of(j * SEGS, SEGS), SEGS)

    sublane = lax.broadcasted_iota(jnp.int32, (SEGS, CH), 0)

    def coefs(k):
        return [jnp.broadcast_to(row_of(rec, g, k), (SEGS, CH)) for g in range(3)]

    def publish(n, A, B):
        SEGT[n, 0] = A
        SEGT[n, 1] = B
        ta, tb = SEGT[n, 0, 0:1], SEGT[n, 1, 0:1]
        for i in range(1, SEGS):
            a, b = SEGT[n, 0, i : i + 1], SEGT[n, 1, i : i + 1]
            ta, tb = a * ta, a * tb + b
        SUM[n] = jnp.where(sublane == 0, ta, tb)

        def one(e, _):
            rcopy(
                SUM.at[n], SLOT.at[n, e], ex_s.at[n], ex_r.at[n], peer(lax.rem(q + e, CHIPS))
            ).start()
            return 0

        lax.fori_loop(1, CHIPS, one, 0)

    def incoming(n, k):
        arrived(SLOT.at[n, pl.ds(1, CHIPS - 1)], ex_r.at[n])

        def one(i, h):
            return SLOT[n, q - i, 0:1] * h + SLOT[n, q - i, 1:2]

        h = lax.fori_loop(0, q, one, row_of(init, 0, k))
        SEGT[n, 2, 0:1] = h
        for i in range(SEGS - 1):
            h = SEGT[n, 0, i : i + 1] * h + SEGT[n, 1, i : i + 1]
            SEGT[n, 2, i + 1 : i + 2] = h
        return SEGT[n, 2]

    UN = 8

    def pass1(k):
        par = k % 2
        coef = coefs(k)
        first = (sublane + q) == 0
        p0 = jnp.where(first, jnp.broadcast_to(row_of(init, 0, k), (SEGS, CH)), 0.0)
        A, B = cell([PRE[par, g, vreg(0), :] for g in range(3)], p0, coef)
        AB1[0, vreg(0), :] = A
        AB1[1, vreg(0), :] = B

        def step(j, A, B):
            a, b = cell_at_zero([PRE[par, g, vreg(j), :] for g in range(3)], coef)
            AB1[0, vreg(j), :] = a
            AB1[1, vreg(j), :] = b
            return a * A, a * B + b

        for j in range(1, UN):
            A, B = step(j, A, B)

        def group(t, AB):
            A, B = AB
            for o in range(UN):
                A, B = step(t * UN + o, A, B)
            return A, B

        A, B = lax.fori_loop(1, SEG // UN, group, (A, B))
        publish(2 * k, A, B)

    def pass2(k):
        par = k % 2
        coef = coefs(k)
        h = incoming(2 * k, k)

        def group(t, carry):
            h, A, B = carry
            for o in range(UN):
                v = vreg(t * UN + o)
                a, b = cell([PRE[par, g, v, :] for g in range(3)], h, coef)
                AB2[0, v, :] = a
                AB2[1, v, :] = b
                h = AB1[0, v, :] * h + AB1[1, v, :]
                A, B = a * A, a * B + b
            return h, A, B

        one, zero = jnp.ones((SEGS, CH), jnp.float32), jnp.zeros((SEGS, CH), jnp.float32)
        _, A, B = lax.fori_loop(0, SEG // UN, group, (h, one, zero))
        publish(2 * k + 1, A, B)

    def pass3(k):
        h = incoming(2 * k + 1, k)

        def group(t, h):
            for o in range(UN):
                j = t * UN + o
                v = vreg(j)
                h = AB2[0, v, :] * h + AB2[1, v, :]
                OUTB[k, pl.ds(j, SEGS, stride=SEG), :] = h
            return h

        lax.fori_loop(0, SEG // UN, group, h)
        here = out_hbm.at[:, chan(c, k)]
        pltpu.make_async_copy(OUTB.at[k, trows(c)], here, o_l.at[k]).start()
        rcopy(OUTB.at[k, trows(1 - c)], here, o_s.at[k], o_r.at[k], sib).start()

    def features_on():
        arrived(X.at[trows(c), tcols(x + 3)], t_r.at[0])
        send(X.at[trows(c, 0), tcols(x + 3)], t_s.at[2], t_r.at[2], xr)
        arrived(X.at[trows(c), tcols(x + 1)], t_r.at[1])
        send(X.at[trows(c, 1), tcols(x + 1)], t_s.at[3], t_r.at[3], xl)
        send(X.at[trows(c), tcols(x + 3)], ts_s.at[1], ts_r.at[1], sib)
        send(X.at[trows(c), tcols(x + 1)], ts_s.at[2], ts_r.at[2], sib)

    def features_end():
        for h in range(2):
            arrived(X.at[trows(c, h), tcols(x + 2)], t_r.at[2 + h])
            send(X.at[trows(c, h), tcols(x + 2)], ts_s.at[3 + h], ts_r.at[3 + h], sib)
        arrived(X.at[trows(1 - c), tcols(x)], ts_r.at[0])
        arrived(X.at[trows(1 - c), tcols(x + 3)], ts_r.at[1])
        arrived(X.at[trows(1 - c), tcols(x + 1)], ts_r.at[2])
        for h in range(2):
            arrived(X.at[trows(1 - c, h), tcols(x + 2)], ts_r.at[3 + h])

    def last_of_group(k):
        for h in range(2):
            arrived(wrows(k, block(p + 2, s), h), p1_r.at[k, 2 + h])
        if k > 0:
            for i in (0, 3, 1):
                send2(k, i)
        send2(k, 2)

    def pass_on(k):
        for i in (0, 3, 1, 2):
            arrived(wrows(k, block(p + i, s + 3)), p2_r.at[k, i, 0])
            send(wrows(k, block(p + i, s + 3), 0), p2_s.at[k, i, 2], p2_r.at[k, i, 2], up)
            arrived(wrows(k, block(p + i, s + 1)), p2_r.at[k, i, 1])
            send(wrows(k, block(p + i, s + 1), 1), p2_s.at[k, i, 3], p2_r.at[k, i, 3], down)

    def gathered(k):
        for i in range(RING):
            for h in range(2):
                arrived(wrows(k, block(p + i, s + 2), h), p2_r.at[k, i, 2 + h])

    last_of_group(0)
    for k in range(CHUNKS + 1):
        if k + 1 < CHUNKS:
            last_of_group(k + 1)
        if k < CHUNKS:
            pass_on(k)
        if k == 0:
            features_on()
        if k == 1:
            features_end()
        if k >= 1:
            gathered(k - 1)
            matmul(k - 1)
            pass1(k - 1)
            if k >= 2:
                pass3(k - 2)
            pass2(k - 1)
    pass3(CHUNKS - 1)

    for k in range(CHUNKS):
        here = out_hbm.at[:, chan(c, k)]
        there = out_hbm.at[:, chan(1 - c, k)]
        arrived(here, o_l.at[k])
        arrived(here, o_s.at[k])
        arrived(there, o_r.at[k])
        arrived(wrows(k, q, 0), sib_s.at[k])
    for ref, sem in sends:
        arrived(ref, sem)
    for n in range(2 * CHUNKS):
        arrived(SLOT.at[n, pl.ds(1, CHIPS - 1)], ex_s.at[n])


def body(tokens, weights, gate_bias, recurrent, initial_state):
    dma = pltpu.SemaphoreType.DMA
    f32, bf16 = jnp.float32, jnp.bfloat16
    vmem, hbm = pl.BlockSpec(memory_space=pltpu.VMEM), pl.BlockSpec(memory_space=pl.ANY)
    return pl.pallas_call(
        kernel,
        out_shape=jax.ShapeDtypeStruct((TOK, 2 * CH * CHUNKS), f32),
        in_specs=[hbm, hbm, vmem, vmem, vmem],
        out_specs=hbm,
        scratch_shapes=[
            pltpu.VMEM((ROWS, DEPTH), bf16),
            pltpu.VMEM((CHUNKS, DEPTH, 3 * CH), bf16),
            pltpu.VMEM((2, 3, ROWS, CH), f32),
            pltpu.VMEM((2, ROWS, CH), f32),
            pltpu.VMEM((2, ROWS, CH), f32),
            pltpu.VMEM((CHUNKS, ROWS, CH), f32),
            pltpu.VMEM((2 * CHUNKS, 3, SEGS, CH), f32),
            pltpu.VMEM((2 * CHUNKS, SEGS, CH), f32),
            pltpu.VMEM((2 * CHUNKS, CHIPS, SEGS, CH), f32),
            dma((CHUNKS + 1,)),
            dma((CHUNKS,)),
            dma((CHUNKS,)),
            dma((CHUNKS, 4)),
            dma((CHUNKS, 4)),
            dma((CHUNKS, RING, 4)),
            dma((CHUNKS, RING, 4)),
            dma((4,)),
            dma((4,)),
            dma((5,)),
            dma((5,)),
            dma((2 * CHUNKS,)),
            dma((2 * CHUNKS,)),
            dma((CHUNKS,)),
            dma((CHUNKS,)),
            dma((CHUNKS,)),
        ],
        compiler_params=pltpu.CompilerParams(
            collective_id=0, has_side_effects=True, vmem_limit_bytes=56 * 2**20
        ),
        cost_estimate=pl.CostEstimate(
            flops=2 * ROWS * DEPTH * 3 * CH * CHUNKS, bytes_accessed=8 * 2**20, transcendentals=0
        ),
    )(tokens, weights, gate_bias, recurrent, initial_state[None, :])


def solution(mesh):
    return jax.shard_map(
        body,
        mesh=mesh,
        in_specs=(P("seq", "tp"), P(None, "seq", "tp"), P(None, "tp"), P(None, "tp"), P("tp")),
        out_specs=P("seq", "tp"),
        check_vma=False,
    )
```

time: 361 us -> 117 us (0.32)
  waiting for transfers between devices: 148 us -> 0 us
  Pallas kernels: 0 us -> 113 us
  blocking collectives: 94.4 us -> 0 us
  other arithmetic: 52.1 us -> 0 us
  local copies, waits for them, and re-layouts: 31.8 us -> 3.16 us
  matrix products: 18 us -> 0 us
  between operations: 14.8 us -> 0.01 us
    all_gather x2 -> x0, waiting for transfers between devices: 147 us -> none  [the longest x1 95.5 us: body(): lax.all_gather(weights, 'seq', axis=1, tiled=True)]
    pallas_call x0 -> x1, Pallas kernels: none -> 113 us  [body(): pl.pallas_call(kernel, out_shape=jax.ShapeDtypeStruct((TOK, 2 * CH * CHUN...]
    all_gather x4 -> x0, blocking collectives: 94.4 us -> none  [prefix(): gathered = jax.tree.map(lambda a: lax.all_gather(a, axis), part)]
    add x31 -> x0, other arithmetic: 29.6 us -> none  [the longest x2 23.8 us: tiled_scan(): run_terms = group_rates[:, inner] * run_terms + group_terms[:, inner]]
    another operation x8 -> x0, local copies, waits for them, and re-layouts: 22 us -> none  [the longest x2 12.6 us: tiled_scan(): inner_terms = jnp.stack(term_list, axis=1)]
    dot_general x1 -> x0, matrix products: 18 us -> none  [body(): jnp.einsum('tk,gkc->gtc', features, lax.all_gather(weights, 'seq', axis=1...]
    mul x22 -> x0, other arithmetic: 13.1 us -> none  [the longest x2 5.84 us: tiled_scan(): products = inner_rates * leading_rates[:, None, :]]
    sub x1 -> x0, other arithmetic: 5.59 us -> none  [body(): offset = stepped - jacobian * previous]
  transfers between devices with their start and end apart: 2 -> 0, of which waited for: 2 -> 0; matrix products, arithmetic and copies ran while one was open for 0% -> 0% of each run, Pallas kernels for 0% -> 0%
where the time goes in v1:
time: 117 us; the launch traced here: 116 us
  Pallas kernels  113 us (97%)
  local copies, waits for them, and re-layouts  3.16 us (3%)
    pallas_call x1, Pallas kernels, body(): pl.pallas_call(kernel, out_shape=jax.ShapeDtypeStruct((TOK, 2 * CH * CHUN...  113 us
    unnamed x1, local copies, waits for them, and re-layouts  3.16 us

profile of v1, /device:TPU:1, one launch (start us, length us, event | category | flops | bytes accessed | tf_op | source)
XLA Modules:
  0.0 116.4 jit_solution(16131718940751759552)
XLA Ops:
  0.0 113.3 %shard_map.55 = f32[512,1024]{1,0:T(8,128)} custom-call(bf16[512,1024]{1,0:T(8,128)(2,1)} %tok_hbm.1, bf16[3,128,1024]{2,1,0:T(8,128)(2,1)} %w_hbm.1, f32[3,1024]{1,0:T(4,128)} %bias.1, f32[3,1024]{1,0:T(4,128)} %rec.1, f32[1,1024]{1,0:T(1,128)} %bitcast.1), custom_call_target="tpu_custom_call" | custom-call | flops 12884901888 | bytes 8388608 | tf_op jit(solution)/shard_map/pallas_call | solution.py:356
  113.3 3.2 %copy.7 = f32[512,1024]{1,0:T(8,128)} copy(f32[512,1024]{1,0:T(8,128)} %shard_map.55) | data formatting | bytes 4194304

commit v2 on v0

v2 whole, which is shorter than its diff:
```python
import functools

import jax
import jax.numpy as jnp
from jax import lax
from jax.experimental import pallas as pl
from jax.experimental.pallas import tpu as pltpu
from jax.sharding import PartitionSpec as P

MESH = pl.DeviceIdType.MESH
RING = 4
CHIPS = RING * RING
CH = 128
WIDTHS = (256, 128, 128)
STARTS = (0, 256, 384)
SUBS = ((0, 1), (2,), (3,))
CHUNKS = len(WIDTHS)
HALF = sum(WIDTHS)
GROUPS = HALF // CH
TOK = 512
ROWS = 2 * TOK
FEAT = 1024
DEPTH = CHIPS * 256
FAR_FIRST = sorted(
    [(i, j) for i in range(RING) for j in range(RING) if i or j],
    key=lambda d: -sum(min(v, RING - v) for v in d),
)
SEGS = 8
SEG = TOK // SEGS


def sigmoid(v):
    return jax.nn.sigmoid(v)


def cell(pre, p, coef):
    u = sigmoid(pre[0] + coef[0] * p)
    r = sigmoid(pre[1] + coef[1] * p)
    c = jnp.tanh(pre[2] + coef[2] * r * p)
    keep = 1.0 - u
    slope = c - p
    jac = (
        keep
        + slope * (u * keep * coef[0])
        + u * ((1.0 - c * c) * coef[2]) * (r + p * (r * (1.0 - r) * coef[1]))
    )
    stepped = keep * p + u * c
    return jac, stepped - jac * p


def cell_at_zero(pre, coef):
    u = sigmoid(pre[0])
    r = sigmoid(pre[1])
    c = jnp.tanh(pre[2])
    keep = 1.0 - u
    jac = keep + c * (u * keep * coef[0]) + u * ((1.0 - c * c) * coef[2]) * r
    return jac, u * c


def kernel(
    tok_hbm, w_hbm, bias, rec, init, out,
    X, W0, W1, W2, PRE, AB1, AB2, OUTB, SEGT, MID, SUM, SLOT,
    local_sem, sib_s, sib_r, w_s, p1_r, p2_r, t_s, t_r, ts_s, ts_r, ex_s, ex_r, o_l, o_s, o_r,
):
    W = (W0, W1, W2)
    ORDER = (0, 3, 1, 2)
    seq, x = lax.axis_index("seq"), lax.axis_index("tp")
    c = lax.rem(seq, 2)
    q = seq // 2
    y, z = q // RING, lax.rem(q, RING)
    p = (1 - c) * y + c * z
    s = (1 - c) * z + c * y

    def block(pp, ss):
        return lax.rem(pp, RING) * (4 - 3 * c) + lax.rem(ss, RING) * (1 + 3 * c)

    def peer(qq):
        return (qq * 2 + c, x)

    right, left = peer(block(p + 1, s)), peer(block(p + 3, s))
    up, down = peer(block(p, s + 1)), peer(block(p, s + 3))
    xr, xl = (seq, lax.rem(x + 1, RING)), (seq, lax.rem(x + 3, RING))
    sib = (q * 2 + 1 - c, x)

    def rcopy(src, dst, ss, rs, dev):
        return pltpu.make_async_remote_copy(
            src_ref=src, dst_ref=dst, send_sem=ss, recv_sem=rs, device_id=dev, device_id_type=MESH
        )

    def send(ref, ss, rs, dev):
        rcopy(ref, ref, ss, rs, dev).start()

    def arrived(ref, sem):
        pltpu.make_async_copy(ref, ref, sem).wait()

    def wrows(k, blk, half=None):
        if half is None:
            return W[k].at[pl.ds(pl.multiple_of(blk * 256, 256), 256)]
        return W[k].at[pl.ds(pl.multiple_of(blk * 256 + half * 128, 128), 128)]

    def chan(core, k):
        return pl.ds(pl.multiple_of(core * HALF + STARTS[k], CH), WIDTHS[k])

    def lanes(core, sub):
        return pl.ds(pl.multiple_of(core * HALF + sub * CH, CH), CH)

    def trows(core, half=None):
        if half is None:
            return pl.ds(pl.multiple_of(core * TOK, TOK), TOK)
        return pl.ds(pl.multiple_of(core * TOK + half * 256, 256), 256)

    def tcols(xx):
        return pl.ds(pl.multiple_of(lax.rem(xx, RING) * FEAT, FEAT), FEAT)

    mine = pl.ds(pl.multiple_of(q * 256 + c * 128, 128), 128)
    own_tok = pltpu.make_async_copy(tok_hbm, X.at[trows(c), tcols(x)], local_sem.at[CHUNKS])
    for k in range(CHUNKS):
        for g in range(3):
            pltpu.make_async_copy(
                w_hbm.at[g, :, chan(c, k)],
                W[k].at[mine, pl.ds(g * WIDTHS[k], WIDTHS[k])],
                local_sem.at[k],
            ).start()
    own_tok.start()

    barrier = pltpu.get_barrier_semaphore()

    def greet(e, _):
        pl.semaphore_signal(
            barrier, inc=1, device_id=peer(lax.rem(q + e, CHIPS)), device_id_type=MESH
        )
        return 0

    lax.fori_loop(1, CHIPS, greet, 0)
    for d in (xr, xl, sib):
        pl.semaphore_signal(barrier, inc=1, device_id=d, device_id_type=MESH)
    pl.semaphore_wait(barrier, CHIPS + 2)

    for k in range(CHUNKS):
        for g in range(3):
            rcopy(
                w_hbm.at[g, :, chan(1 - c, k)],
                W[k].at[mine, pl.ds(g * WIDTHS[k], WIDTHS[k])],
                sib_s.at[k], sib_r.at[k], sib,
            ).start()
        arrived(wrows(k, q, c), local_sem.at[k])
        send(wrows(k, q, c), w_s.at[k], p1_r.at[k, 0], right)
        send(wrows(k, q, c), w_s.at[k], p1_r.at[k, 1], left)
    own_tok.wait()
    for h in range(2):
        send(X.at[trows(c, h), tcols(x)], t_s.at[0, h], t_r.at[0, h], xr)
        send(X.at[trows(c, 1 - h), tcols(x)], t_s.at[1, 1 - h], t_r.at[1, 1 - h], xl)
    send(X.at[trows(c), tcols(x)], ts_s.at[0], ts_r.at[0], sib)

    def send2(k, i):
        own = block(p + i, s)
        send(wrows(k, own, 0), w_s.at[k], p2_r.at[k, i, 0], up)
        send(wrows(k, own, 1), w_s.at[k], p2_r.at[k, i, 1], down)

    def send2b(k, i):
        own = block(p + i, s)
        send(wrows(k, own, 1), w_s.at[k], p2_r.at[k, i, 4], up)
        send(wrows(k, own, 0), w_s.at[k], p2_r.at[k, i, 5], down)

    def sibling_rows(k):
        arrived(wrows(k, q, 1 - c), sib_r.at[k])
        send(wrows(k, q, 1 - c), w_s.at[k], p1_r.at[k, 2], right)
        send(wrows(k, q, 1 - c), w_s.at[k], p1_r.at[k, 3], left)

    def ring_on(k):
        arrived(wrows(k, block(p + 3, s), c), p1_r.at[k, 0])
        send(wrows(k, block(p + 3, s), c), w_s.at[k], p1_r.at[k, 4], right)
        arrived(wrows(k, block(p + 1, s), c), p1_r.at[k, 1])
        arrived(wrows(k, block(p + 1, s), 1 - c), p1_r.at[k, 3])
        send(wrows(k, block(p + 1, s), 1 - c), w_s.at[k], p1_r.at[k, 5], left)
        arrived(wrows(k, block(p + 3, s), 1 - c), p1_r.at[k, 2])

    def ring_end(k):
        arrived(wrows(k, block(p + 2, s), c), p1_r.at[k, 4])
        arrived(wrows(k, block(p + 2, s), 1 - c), p1_r.at[k, 5])

    def pass_on(k, i):
        below, above = block(p + i, s + 3), block(p + i, s + 1)
        arrived(wrows(k, below, 0), p2_r.at[k, i, 0])
        send(wrows(k, below, 0), w_s.at[k], p2_r.at[k, i, 2], up)
        arrived(wrows(k, above, 1), p2_r.at[k, i, 1])
        send(wrows(k, above, 1), w_s.at[k], p2_r.at[k, i, 3], down)

    def near(k, i):
        arrived(wrows(k, block(p + i, s + 3), 1), p2_r.at[k, i, 4])
        arrived(wrows(k, block(p + i, s + 1), 0), p2_r.at[k, i, 5])

    def far(k, i):
        for h in range(2):
            arrived(wrows(k, block(p + i, s + 2), h), p2_r.at[k, i, 2 + h])

    def gathered(k):
        for i in ORDER:
            near(k, i)
            far(k, i)

    def features_first():
        arrived(X.at[trows(c, 0), tcols(x + 3)], t_r.at[0, 0])
        send(X.at[trows(c, 0), tcols(x + 3)], t_s.at[2, 0], t_r.at[2, 0], xr)
        arrived(X.at[trows(c, 1), tcols(x + 1)], t_r.at[1, 1])
        send(X.at[trows(c, 1), tcols(x + 1)], t_s.at[2, 1], t_r.at[2, 1], xl)
        send(X.at[trows(c, 0), tcols(x + 3)], ts_s.at[1], ts_r.at[1], sib)
        send(X.at[trows(c, 1), tcols(x + 1)], ts_s.at[2], ts_r.at[2], sib)

    def features_second():
        arrived(X.at[trows(c, 1), tcols(x + 3)], t_r.at[0, 1])
        send(X.at[trows(c, 1), tcols(x + 3)], ts_s.at[3], ts_r.at[3], sib)
        arrived(X.at[trows(c, 0), tcols(x + 1)], t_r.at[1, 0])
        send(X.at[trows(c, 0), tcols(x + 1)], ts_s.at[4], ts_r.at[4], sib)

    def features_end():
        for h in range(2):
            arrived(X.at[trows(c, h), tcols(x + 2)], t_r.at[2, h])
            send(X.at[trows(c, h), tcols(x + 2)], ts_s.at[5 + h], ts_r.at[5 + h], sib)
        arrived(X.at[trows(1 - c), tcols(x)], ts_r.at[0])
        for n, (h, d) in enumerate(((0, 3), (1, 1), (1, 3), (0, 1), (0, 2), (1, 2))):
            arrived(X.at[trows(1 - c, h), tcols(x + d)], ts_r.at[1 + n])

    def row_of(ref, g, sub):
        return ref[pl.ds(g, 1), lanes(c, sub)]

    def put(k, acc, t, add):
        m = c if t < 2 else 1 - c
        for n, sub in enumerate(SUBS[k]):
            for g in range(3):
                v = acc[:, g * WIDTHS[k] + n * CH : g * WIDTHS[k] + (n + 1) * CH]
                if not add:
                    v = v + row_of(bias, g, sub)
                for h in range(SEGS // 2):
                    at = pl.ds((t % 2) * (SEGS // 2) + h, SEG, stride=SEGS)
                    part = v[h * SEG : (h + 1) * SEG]
                    PRE[sub, g, m, at, :] = PRE[sub, g, m, at, :] + part if add else part

    def quarter(t):
        return trows(c if t < 2 else 1 - c, t % 2)

    def matmul(k, t):
        acc = jnp.dot(X[quarter(t), :], W[k][...], preferred_element_type=jnp.float32)
        put(k, acc, t, False)

    def matmul_part(k, t, places, add):
        at = [
            pl.ds(pl.multiple_of(block(p + i, s + o) * 256, 256), 256)
            for i in places
            for o in range(RING)
        ]
        a = jnp.concatenate([X[quarter(t), d] for d in at], axis=1)
        b = jnp.concatenate([W[k][d, :] for d in at], axis=0)
        put(k, jnp.dot(a, b, preferred_element_type=jnp.float32), t, add)

    def vreg(j):
        return pl.ds(pl.multiple_of(j * SEGS, SEGS), SEGS)

    sublane = lax.broadcasted_iota(jnp.int32, (SEGS, CH), 0)

    def coefs(sub):
        return [jnp.broadcast_to(row_of(rec, g, sub), (SEGS, CH)) for g in range(3)]

    def publish(n, sub, AB):
        tot = []
        for m in range(2):
            SEGT[n, sub, m, 0], SEGT[n, sub, m, 1] = AB[m]
            ta, tb = SEGT[n, sub, m, 0, 0:1], SEGT[n, sub, m, 1, 0:1]
            for i in range(1, SEGS):
                a, b = SEGT[n, sub, m, 0, i : i + 1], SEGT[n, sub, m, 1, i : i + 1]
                ta, tb = a * ta, a * tb + b
            tot.append((ta, tb))
        (a0, b0), (a1, b1) = tot
        MID[n, sub] = jnp.where(sublane == 0, a0, b0)
        SUM[n, sub] = jnp.where(sublane == 0, a0 * a1, a1 * b0 + b1)

    def span(k):
        return pl.ds(SUBS[k][0], len(SUBS[k]))

    def exchange(n, k):
        for dy, dz in FAR_FIRST:
            there = lax.rem(y + dy, RING) * RING + lax.rem(z + dz, RING)
            rcopy(
                SUM.at[n, span(k)], SLOT.at[n, lax.rem(there - q + CHIPS, CHIPS), span(k)],
                ex_s.at[n, k], ex_r.at[n, k], peer(there),
            ).start()

    def exchanged(n, k, sem):
        arrived(SLOT.at[n, pl.ds(1, CHIPS - 1), span(k)], sem.at[n, k])

    def incoming(n, sub):
        h = row_of(init, 0, sub)
        for e in range(CHIPS - 1, 0, -1):
            h = jnp.where(e <= q, SLOT[n, e, sub, 0:1] * h + SLOT[n, e, sub, 1:2], h)
        starts = [h, MID[n, sub, 0:1] * h + MID[n, sub, 1:2]]
        for m in range(2):
            h = starts[m]
            SEGT[n, sub, m, 2, 0:1] = h
            for i in range(SEGS - 1):
                h = SEGT[n, sub, m, 0, i : i + 1] * h + SEGT[n, sub, m, 1, i : i + 1]
                SEGT[n, sub, m, 2, i + 1 : i + 2] = h
        return [SEGT[n, sub, m, 2] for m in range(2)]

    UN = 4

    def pass1(sub):
        coef = coefs(sub)
        first = (sublane + q) == 0
        p0 = jnp.where(first, jnp.broadcast_to(row_of(init, 0, sub), (SEGS, CH)), 0.0)

        def step(j, AB, p0=None):
            new = []
            for m in range(2):
                v = vreg(j)
                pre = [PRE[sub, g, m, v, :] for g in range(3)]
                a, b = cell_at_zero(pre, coef) if p0 is None or m else cell(pre, p0, coef)
                AB1[sub, 0, m, v, :] = a
                AB1[sub, 1, m, v, :] = b
                new.append((a, b) if AB is None else (a * AB[m][0], a * AB[m][1] + b))
            return new

        AB = step(0, None, p0)
        for j in range(1, UN):
            AB = step(j, AB)

        def group(t, AB):
            for o in range(UN):
                AB = step(t * UN + o, AB)
            return AB

        publish(0, sub, lax.fori_loop(1, SEG // UN, group, AB))

    def pass2(sub):
        coef = coefs(sub)

        def group(t, carry):
            for o in range(UN):
                v = vreg(t * UN + o)
                new = []
                for m in range(2):
                    h, A, B = carry[m]
                    a, b = cell([PRE[sub, g, m, v, :] for g in range(3)], h, coef)
                    AB2[sub, 0, m, v, :] = a
                    AB2[sub, 1, m, v, :] = b
                    h = AB1[sub, 0, m, v, :] * h + AB1[sub, 1, m, v, :]
                    new.append((h, a * A, a * B + b))
                carry = new
            return carry

        one, zero = jnp.ones((SEGS, CH), jnp.float32), jnp.zeros((SEGS, CH), jnp.float32)
        carry = lax.fori_loop(0, SEG // UN, group, [(h, one, zero) for h in incoming(0, sub)])
        publish(1, sub, [(A, B) for _, A, B in carry])

    def pass3(sub):
        def group(t, hs):
            for o in range(UN):
                j = t * UN + o
                v = vreg(j)
                hs = [AB2[sub, 0, m, v, :] * hs[m] + AB2[sub, 1, m, v, :] for m in range(2)]
                for m in range(2):
                    OUTB[sub, pl.ds(m * TOK + j, SEGS, stride=SEG), :] = hs[m]
            return hs

        lax.fori_loop(0, SEG // UN, group, incoming(1, sub))
        here = out.at[:, lanes(c, sub)]
        rcopy(OUTB.at[sub, trows(1 - c)], here, o_s.at[sub], o_r.at[sub], sib).start()
        pltpu.make_async_copy(OUTB.at[sub, trows(c)], here, o_l.at[sub]).start()

    def put_out(sub):
        here, there = out.at[:, lanes(c, sub)], out.at[:, lanes(1 - c, sub)]
        arrived(here, o_l.at[sub])
        arrived(here, o_s.at[sub])
        arrived(there, o_r.at[sub])

    def first_pass(k):
        for sub in SUBS[k]:
            pass1(sub)
        exchange(0, k)

    def second_pass(k, between=()):
        exchanged(0, k, ex_r)
        for n, sub in enumerate(SUBS[k]):
            pass2(sub)
            if n < len(between):
                pass_on(2, between[n])
        exchange(1, k)

    def last_pass(k):
        exchanged(1, k, ex_r)
        for sub in SUBS[k]:
            pass3(sub)

    def sent(k):
        arrived(wrows(k, q, c), sib_s.at[k])
        arrived(W[k].at[pl.ds(0, 30 * 128)], w_s.at[k])

    def sent_features():
        for h in range(2):
            for d in range(3):
                arrived(X.at[trows(c, h), tcols(x)], t_s.at[d, h])
        arrived(X.at[trows(c), tcols(x)], ts_s.at[0])
        for n in range(6):
            arrived(X.at[trows(c, 0), tcols(x)], ts_s.at[1 + n])

    for k in range(CHUNKS):
        sibling_rows(k)
        if k == 0:
            send2(0, 0)
    for k in range(CHUNKS):
        ring_on(k)
        if k == 0:
            send2(0, 3)
            send2(0, 1)
            send2b(0, 0)
    features_first()
    ring_end(0)
    send2(0, 2)
    ring_end(1)
    ring_end(2)
    send2b(0, 3)
    send2b(0, 1)
    send2b(0, 2)
    pass_on(0, 0)
    pass_on(0, 3)
    send2(1, 0)
    features_second()
    pass_on(0, 1)
    send2(1, 3)
    pass_on(0, 2)
    send2(1, 1)
    send2(1, 2)
    for i in ORDER:
        send2b(1, i)
    features_end()
    gathered(0)
    send2(2, 0)
    send2b(2, 0)
    for t in range(4):
        matmul(0, t)
        pass_on(1, ORDER[t])
        if t == 2:
            send2(2, 3)
            send2b(2, 3)
    for i in (1, 2):
        send2(2, i)
        send2b(2, i)
    first_pass(0)
    pass_on(2, 0)
    gathered(1)
    for t in range(4):
        matmul(1, t)
        if t == 1:
            pass_on(2, 3)
    pass_on(2, 1)
    first_pass(1)
    second_pass(0, (2,))
    for i in (0, 3, 1):
        near(2, i)
        far(2, i)
    for t in range(4):
        matmul_part(2, t, (0, 3, 1), False)
    second_pass(1)
    sent(0)
    sent(1)
    sent_features()
    near(2, 2)
    far(2, 2)
    for t in range(4):
        matmul_part(2, t, (2,), True)
    first_pass(2)
    last_pass(0)
    last_pass(1)
    sent(2)
    for k in range(CHUNKS - 1):
        exchanged(0, k, ex_s)
        exchanged(1, k, ex_s)
    second_pass(2)
    for k in range(CHUNKS - 1):
        for sub in SUBS[k]:
            put_out(sub)
    exchanged(0, 2, ex_s)
    last_pass(2)
    exchanged(1, 2, ex_s)
    put_out(SUBS[2][0])


def body(tokens, weights, gate_bias, recurrent, initial_state):
    dma = pltpu.SemaphoreType.DMA
    f32, bf16 = jnp.float32, jnp.bfloat16
    vmem, hbm = pl.BlockSpec(memory_space=pltpu.VMEM), pl.BlockSpec(memory_space=pl.ANY)
    return pl.pallas_call(
        kernel,
        out_shape=jax.ShapeDtypeStruct((TOK, 2 * HALF), f32),
        in_specs=[hbm, hbm, vmem, vmem, vmem],
        out_specs=hbm,
        scratch_shapes=[
            pltpu.VMEM((ROWS, DEPTH), bf16),
            *[pltpu.VMEM((DEPTH, 3 * w), bf16) for w in WIDTHS],
            pltpu.VMEM((GROUPS, 3, 2, TOK, CH), f32),
            pltpu.VMEM((GROUPS, 2, 2, TOK, CH), f32),
            pltpu.VMEM((GROUPS, 2, 2, TOK, CH), f32),
            pltpu.VMEM((GROUPS, ROWS, CH), f32),
            pltpu.VMEM((2, GROUPS, 2, 3, SEGS, CH), f32),
            pltpu.VMEM((2, GROUPS, SEGS, CH), f32),
            pltpu.VMEM((2, GROUPS, SEGS, CH), f32),
            pltpu.VMEM((2, CHIPS, GROUPS, SEGS, CH), f32),
            dma((CHUNKS + 1,)),
            dma((CHUNKS,)),
            dma((CHUNKS,)),
            dma((CHUNKS,)),
            dma((CHUNKS, 6)),
            dma((CHUNKS, RING, 6)),
            dma((3, 2)),
            dma((3, 2)),
            dma((7,)),
            dma((7,)),
            dma((2, CHUNKS)),
            dma((2, CHUNKS)),
            dma((GROUPS,)),
            dma((GROUPS,)),
            dma((GROUPS,)),
        ],
        compiler_params=pltpu.CompilerParams(
            collective_id=0, has_side_effects=True, vmem_limit_bytes=56 * 2**20
        ),
        cost_estimate=pl.CostEstimate(
            flops=2 * ROWS * DEPTH * 3 * HALF, bytes_accessed=8 * 2**20, transcendentals=0
        ),
    )(tokens, weights, gate_bias, recurrent, initial_state[None, :])


def solution(mesh):
    return jax.shard_map(
        body,
        mesh=mesh,
        in_specs=(P("seq", "tp"), P(None, "seq", "tp"), P(None, "tp"), P(None, "tp"), P("tp")),
        out_specs=P("seq", "tp"),
        check_vma=False,
    )
```

time: 361 us -> 101 us (0.28)
  waiting for transfers between devices: 148 us -> 0 us
  Pallas kernels: 0 us -> 97.3 us
  blocking collectives: 94.4 us -> 0 us
  other arithmetic: 52.1 us -> 0 us
  local copies, waits for them, and re-layouts: 31.8 us -> 3.16 us
  matrix products: 18 us -> 0 us
  between operations: 14.8 us -> 0.01 us
    all_gather x2 -> x0, waiting for transfers between devices: 147 us -> none  [the longest x1 95.5 us: body(): lax.all_gather(weights, 'seq', axis=1, tiled=True)]
    pallas_call x0 -> x1, Pallas kernels: none -> 97.3 us  [body(): pl.pallas_call(kernel, out_shape=jax.ShapeDtypeStruct((TOK, 2 * HALF), f3...]
    all_gather x4 -> x0, blocking collectives: 94.4 us -> none  [prefix(): gathered = jax.tree.map(lambda a: lax.all_gather(a, axis), part)]
    add x31 -> x0, other arithmetic: 29.6 us -> none  [the longest x2 23.8 us: tiled_scan(): run_terms = group_rates[:, inner] * run_terms + group_terms[:, inner]]
    another operation x8 -> x0, local copies, waits for them, and re-layouts: 22 us -> none  [the longest x2 12.6 us: tiled_scan(): inner_terms = jnp.stack(term_list, axis=1)]
    dot_general x1 -> x0, matrix products: 18 us -> none  [body(): jnp.einsum('tk,gkc->gtc', features, lax.all_gather(weights, 'seq', axis=1...]
    mul x22 -> x0, other arithmetic: 13.1 us -> none  [the longest x2 5.84 us: tiled_scan(): products = inner_rates * leading_rates[:, None, :]]
    sub x1 -> x0, other arithmetic: 5.59 us -> none  [body(): offset = stepped - jacobian * previous]
  transfers between devices with their start and end apart: 2 -> 0, of which waited for: 2 -> 0; matrix products, arithmetic and copies ran while one was open for 0% -> 0% of each run, Pallas kernels for 0% -> 0%
where the time goes in v2:
time: 101 us; the launch traced here: 100 us
  Pallas kernels  97.3 us (96%)
  local copies, waits for them, and re-layouts  3.16 us (3%)
    pallas_call x1, Pallas kernels, body(): pl.pallas_call(kernel, out_shape=jax.ShapeDtypeStruct((TOK, 2 * HALF), f3...  97.3 us
    unnamed x1, local copies, waits for them, and re-layouts  3.16 us

profile of v2, /device:TPU:1, one launch (start us, length us, event | category | flops | bytes accessed | tf_op | source)
XLA Modules:
  0.0 100.4 jit_solution(13713392474005485404)
XLA Ops:
  0.0 97.3 %shard_map.55 = f32[512,1024]{1,0:T(8,128)} custom-call(bf16[512,1024]{1,0:T(8,128)(2,1)} %tok_hbm.1, bf16[3,128,1024]{2,1,0:T(8,128)(2,1)} %w_hbm.1, f32[3,1024]{1,0:T(4,128)} %bias.1, f32[3,1024]{1,0:T(4,128)} %rec.1, f32[1,1024]{1,0:T(1,128)} %bitcast.1), custom_call_target="tpu_custom_call" | custom-call | flops 12884901888 | bytes 8388608 | tf_op jit(solution)/shard_map/pallas_call | solution.py:491
  97.3 3.2 %copy.7 = f32[512,1024]{1,0:T(8,128)} copy(f32[512,1024]{1,0:T(8,128)} %shard_map.55) | data formatting | bytes 4194304

commit v3 on v2

--- a/solution.py
+++ b/solution.py
@@ -125,16 +125,9 @@
 
     barrier = pltpu.get_barrier_semaphore()
 
-    def greet(e, _):
-        pl.semaphore_signal(
-            barrier, inc=1, device_id=peer(lax.rem(q + e, CHIPS)), device_id_type=MESH
-        )
-        return 0
-
-    lax.fori_loop(1, CHIPS, greet, 0)
-    for d in (xr, xl, sib):
+    for d in (right, left, up, down, xr, xl, sib):
         pl.semaphore_signal(barrier, inc=1, device_id=d, device_id_type=MESH)
-    pl.semaphore_wait(barrier, CHIPS + 2)
+    pl.semaphore_wait(barrier, 7)
 
     for k in range(CHUNKS):
         for g in range(3):
@@ -243,12 +236,8 @@
         acc = jnp.dot(X[quarter(t), :], W[k][...], preferred_element_type=jnp.float32)
         put(k, acc, t, False)
 
-    def matmul_part(k, t, places, add):
-        at = [
-            pl.ds(pl.multiple_of(block(p + i, s + o) * 256, 256), 256)
-            for i in places
-            for o in range(RING)
-        ]
+    def matmul_part(k, t, chips, add):
+        at = [pl.ds(pl.multiple_of(block(p + i, s + o) * 256, 256), 256) for i, o in chips]
         a = jnp.concatenate([X[quarter(t), d] for d in at], axis=1)
         b = jnp.concatenate([W[k][d, :] for d in at], axis=0)
         put(k, jnp.dot(a, b, preferred_element_type=jnp.float32), t, add)
@@ -445,50 +434,76 @@
         send2(2, i)
         send2b(2, i)
     first_pass(0)
-    pass_on(2, 0)
-    gathered(1)
+    for i in ORDER:
+        near(1, i)
     for t in range(4):
-        matmul(1, t)
-        if t == 1:
-            pass_on(2, 3)
+        matmul_part(1, t, [(i, o) for o in (0, 1, 3) for i in ORDER], False)
+        if t % 2 == 1:
+            pass_on(2, ORDER[t // 2])
+    for i in ORDER:
+        far(1, i)
+    for t in range(4):
+        matmul_part(1, t, [(i, 2) for i in ORDER], True)
+    first_pass(1)
     pass_on(2, 1)
-    first_pass(1)
     second_pass(0, (2,))
-    for i in (0, 3, 1):
+    for i in ORDER:
         near(2, i)
-        far(2, i)
     for t in range(4):
-        matmul_part(2, t, (0, 3, 1), False)
+        matmul_part(2, t, [(i, o) for o in (0, 1, 3) for i in ORDER], False)
+    far(2, 0)
+    far(2, 3)
+    for t in range(4):
+        matmul_part(2, t, [(i, 2) for i in (0, 3)], True)
+    far(2, 1)
+    far(2, 2)
+    for t in range(4):
+        matmul_part(2, t, [(i, 2) for i in (1, 2)], True)
+    first_pass(2)
     second_pass(1)
+    last_pass(0)
     sent(0)
     sent(1)
-    sent_features()
-    near(2, 2)
-    far(2, 2)
-    for t in range(4):
-        matmul_part(2, t, (2,), True)
-    first_pass(2)
-    last_pass(0)
+    second_pass(2)
     last_pass(1)
     sent(2)
-    for k in range(CHUNKS - 1):
+    sent_features()
+    for k in range(CHUNKS):
         exchanged(0, k, ex_s)
-        exchanged(1, k, ex_s)
-    second_pass(2)
+    exchanged(1, 0, ex_s)
+    exchanged(1, 1, ex_s)
     for k in range(CHUNKS - 1):
         for sub in SUBS[k]:
             put_out(sub)
-    exchanged(0, 2, ex_s)
     last_pass(2)
     exchanged(1, 2, ex_s)
     put_out(SUBS[2][0])
+
+
+def copy_out(src, dst, buf, load, store):
+    rows = TOK // 8
+    ins = [
+        pltpu.make_async_copy(src.at[pl.ds(i * rows, rows)], buf.at[pl.ds(i * rows, rows)], load.at[i])
+        for i in range(8)
+    ]
+    outs = [
+        pltpu.make_async_copy(buf.at[pl.ds(i * rows, rows)], dst.at[pl.ds(i * rows, rows)], store.at[i])
+        for i in range(8)
+    ]
+    for cp in ins:
+        cp.start()
+    for cp, nxt in zip(ins, outs):
+        cp.wait()
+        nxt.start()
+    for cp in outs:
+        cp.wait()
 
 
 def body(tokens, weights, gate_bias, recurrent, initial_state):
     dma = pltpu.SemaphoreType.DMA
     f32, bf16 = jnp.float32, jnp.bfloat16
     vmem, hbm = pl.BlockSpec(memory_space=pltpu.VMEM), pl.BlockSpec(memory_space=pl.ANY)
-    return pl.pallas_call(
+    states = pl.pallas_call(
         kernel,
         out_shape=jax.ShapeDtypeStruct((TOK, 2 * HALF), f32),
         in_specs=[hbm, hbm, vmem, vmem, vmem],
@@ -527,6 +542,14 @@
             flops=2 * ROWS * DEPTH * 3 * HALF, bytes_accessed=8 * 2**20, transcendentals=0
         ),
     )(tokens, weights, gate_bias, recurrent, initial_state[None, :])
+    return pl.pallas_call(
+        copy_out,
+        out_shape=jax.ShapeDtypeStruct((TOK, 2 * HALF), f32),
+        in_specs=[hbm],
+        out_specs=hbm,
+        scratch_shapes=[pltpu.VMEM((TOK, 2 * HALF), f32), dma((8,)), dma((8,))],
+        compiler_params=pltpu.CompilerParams(vmem_limit_bytes=56 * 2**20),
+    )(states)
 
 
 def solution(mesh):

time: 101 us -> 97.5 us (0.965)
  local copies, waits for them, and re-layouts: 3.16 us -> 0 us
    unnamed x1 -> x0, local copies, waits for them, and re-layouts: 3.16 us -> none
    pallas_call x1, Pallas kernels: 97.3 us -> 94.8 us  [body(): pl.pallas_call(kernel, out_shape=jax.ShapeDtypeStruct((TOK, 2 * HALF), f3...]
    pallas_call x0 -> x1, Pallas kernels: none -> 2.39 us  [body(): pl.pallas_call(copy_out, out_shape=jax.ShapeDtypeStruct((TOK, 2 * HALF),...]
where the time goes in v3:
time: 97.5 us; the launch traced here: 97.4 us
  Pallas kernels  97.2 us (100%)
    pallas_call x1, Pallas kernels, body(): pl.pallas_call(kernel, out_shape=jax.ShapeDtypeStruct((TOK, 2 * HALF), f3...  94.8 us
    pallas_call x1, Pallas kernels, body(): pl.pallas_call(copy_out, out_shape=jax.ShapeDtypeStruct((TOK, 2 * HALF),...  2.39 us

profile of v3, /device:TPU:1, one launch (start us, length us, event | category | flops | bytes accessed | tf_op | source)
XLA Modules:
  0.0 97.4 jit_solution(15542627466314587313)
XLA Ops:
  0.0 94.8 %shard_map.55.src = f32[512,1024]{1,0:T(8,128)} custom-call(bf16[512,1024]{1,0:T(8,128)(2,1)} %tok_hbm.1, bf16[3,128,1024]{2,1,0:T(8,128)(2,1)} %w_hbm.1, f32[3,1024]{1,0:T(4,128)} %bias.1, f32[3,1024]{1,0:T(4,128)} %rec.1, f32[1,1024]{1,0:T(1,128)} %bitcast.1), custom_call_target="tpu_custom_call" | custom-call | flops 12884901888 | bytes 8388608 | tf_op jit(solution)/shard_map/pallas_call | solution.py:506
  94.8 2.4 %shard_map.56 = f32[512,1024]{1,0:T(8,128)} custom-call(f32[512,1024]{1,0:T(8,128)} %shard_map.55.src), custom_call_target="tpu_custom_call" | custom-call | tf_op jit(solution)/shard_map/pallas_call | solution.py:545

commit v4 on v3

--- a/solution.py
+++ b/solution.py
@@ -17,6 +17,7 @@
 CHUNKS = len(WIDTHS)
 HALF = sum(WIDTHS)
 GROUPS = HALF // CH
+PASSES = ((0, 3), (3, 1))
 TOK = 512
 ROWS = 2 * TOK
 FEAT = 1024
@@ -129,6 +130,11 @@
         pl.semaphore_signal(barrier, inc=1, device_id=d, device_id_type=MESH)
     pl.semaphore_wait(barrier, 7)
 
+    def own_rows(k):
+        arrived(wrows(k, q, c), local_sem.at[k])
+        send(wrows(k, q, c), w_s.at[k], p1_r.at[k, 0], right)
+        send(wrows(k, q, c), w_s.at[k], p1_r.at[k, 1], left)
+
     for k in range(CHUNKS):
         for g in range(3):
             rcopy(
@@ -136,9 +142,8 @@
                 W[k].at[mine, pl.ds(g * WIDTHS[k], WIDTHS[k])],
                 sib_s.at[k], sib_r.at[k], sib,
             ).start()
-        arrived(wrows(k, q, c), local_sem.at[k])
-        send(wrows(k, q, c), w_s.at[k], p1_r.at[k, 0], right)
-        send(wrows(k, q, c), w_s.at[k], p1_r.at[k, 1], left)
+        if k == 0:
+            own_rows(0)
     own_tok.wait()
     for h in range(2):
         send(X.at[trows(c, h), tcols(x)], t_s.at[0, h], t_r.at[0, h], xr)
@@ -206,13 +211,19 @@
         arrived(X.at[trows(c, 0), tcols(x + 1)], t_r.at[1, 0])
         send(X.at[trows(c, 0), tcols(x + 1)], ts_s.at[4], ts_r.at[4], sib)
 
-    def features_end():
+    def features_last():
         for h in range(2):
             arrived(X.at[trows(c, h), tcols(x + 2)], t_r.at[2, h])
             send(X.at[trows(c, h), tcols(x + 2)], ts_s.at[5 + h], ts_r.at[5 + h], sib)
+
+    def sibling_features():
         arrived(X.at[trows(1 - c), tcols(x)], ts_r.at[0])
-        for n, (h, d) in enumerate(((0, 3), (1, 1), (1, 3), (0, 1), (0, 2), (1, 2))):
+        for n, (h, d) in enumerate(((0, 3), (1, 1), (1, 3), (0, 1))):
             arrived(X.at[trows(1 - c, h), tcols(x + d)], ts_r.at[1 + n])
+
+    def sibling_last():
+        for h in range(2):
+            arrived(X.at[trows(1 - c, h), tcols(x + 2)], ts_r.at[5 + h])
 
     def row_of(ref, g, sub):
         return ref[pl.ds(g, 1), lanes(c, sub)]
@@ -232,9 +243,11 @@
     def quarter(t):
         return trows(c if t < 2 else 1 - c, t % 2)
 
-    def matmul(k, t):
-        acc = jnp.dot(X[quarter(t), :], W[k][...], preferred_element_type=jnp.float32)
-        put(k, acc, t, False)
+    def matmul(k, t, places, add):
+        cols = [tcols(x + d) for d in places]
+        a = jnp.concatenate([X[quarter(t), d] for d in cols], axis=1)
+        b = jnp.concatenate([W[k][d, :] for d in cols], axis=0)
+        put(k, jnp.dot(a, b, preferred_element_type=jnp.float32), t, add)
 
     def matmul_part(k, t, chips, add):
         at = [pl.ds(pl.multiple_of(block(p + i, s + o) * 256, 256), 256) for i, o in chips]
@@ -264,7 +277,7 @@
         SUM[n, sub] = jnp.where(sublane == 0, a0 * a1, a1 * b0 + b1)
 
     def span(k):
-        return pl.ds(SUBS[k][0], len(SUBS[k]))
+        return pl.ds(*PASSES[k])
 
     def exchange(n, k):
         for dy, dz in FAR_FIRST:
@@ -290,7 +303,7 @@
                 SEGT[n, sub, m, 2, i + 1 : i + 2] = h
         return [SEGT[n, sub, m, 2] for m in range(2)]
 
-    UN = 4
+    UN = 16
 
     def pass1(sub):
         coef = coefs(sub)
@@ -364,19 +377,18 @@
     def first_pass(k):
         for sub in SUBS[k]:
             pass1(sub)
-        exchange(0, k)
-
-    def second_pass(k, between=()):
+        if k > 0:
+            exchange(0, k - 1)
+
+    def second_pass(k):
         exchanged(0, k, ex_r)
-        for n, sub in enumerate(SUBS[k]):
+        for sub in range(PASSES[k][0], sum(PASSES[k])):
             pass2(sub)
-            if n < len(between):
-                pass_on(2, between[n])
         exchange(1, k)
 
     def last_pass(k):
         exchanged(1, k, ex_r)
-        for sub in SUBS[k]:
+        for sub in range(PASSES[k][0], sum(PASSES[k])):
             pass3(sub)
 
     def sent(k):
@@ -391,49 +403,57 @@
         for n in range(6):
             arrived(X.at[trows(c, 0), tcols(x)], ts_s.at[1 + n])
 
-    for k in range(CHUNKS):
-        sibling_rows(k)
-        if k == 0:
-            send2(0, 0)
-    for k in range(CHUNKS):
-        ring_on(k)
-        if k == 0:
-            send2(0, 3)
-            send2(0, 1)
-            send2b(0, 0)
-    features_first()
+    sibling_rows(0)
+    send2(0, 0)
+    send2b(0, 0)
+    ring_on(0)
+    for i in (3, 1):
+        send2(0, i)
+        send2b(0, i)
     ring_end(0)
     send2(0, 2)
-    ring_end(1)
-    ring_end(2)
-    send2b(0, 3)
-    send2b(0, 1)
     send2b(0, 2)
+    features_first()
     pass_on(0, 0)
     pass_on(0, 3)
-    send2(1, 0)
+    own_rows(1)
+    sibling_rows(1)
+    pass_on(0, 1)
+    pass_on(0, 2)
     features_second()
-    pass_on(0, 1)
-    send2(1, 3)
-    pass_on(0, 2)
-    send2(1, 1)
-    send2(1, 2)
+    ring_on(1)
+    ring_end(1)
     for i in ORDER:
+        send2(1, i)
         send2b(1, i)
-    features_end()
+    own_rows(2)
+    sibling_rows(2)
     gathered(0)
+    matmul(0, 0, (0, 3, 1), False)
+    ring_on(2)
+    matmul(0, 1, (0, 3, 1), False)
+    ring_end(2)
     send2(2, 0)
     send2b(2, 0)
-    for t in range(4):
-        matmul(0, t)
-        pass_on(1, ORDER[t])
-        if t == 2:
-            send2(2, 3)
-            send2b(2, 3)
+    pass_on(1, 0)
+    sibling_features()
+    matmul(0, 2, (0, 3, 1), False)
+    features_last()
+    pass_on(1, 3)
+    matmul(0, 3, (0, 3, 1), False)
+    pass_on(1, 1)
+    send2(2, 3)
+    send2b(2, 3)
+    matmul(0, 0, (2,), True)
+    matmul(0, 1, (2,), True)
+    pass_on(1, 2)
+    sibling_last()
+    matmul(0, 2, (2,), True)
+    matmul(0, 3, (2,), True)
+    first_pass(0)
     for i in (1, 2):
         send2(2, i)
         send2b(2, i)
-    first_pass(0)
     for i in ORDER:
         near(1, i)
     for t in range(4):
@@ -446,7 +466,7 @@
         matmul_part(1, t, [(i, 2) for i in ORDER], True)
     first_pass(1)
     pass_on(2, 1)
-    second_pass(0, (2,))
+    pass_on(2, 2)
     for i in ORDER:
         near(2, i)
     for t in range(4):
@@ -460,24 +480,19 @@
     for t in range(4):
         matmul_part(2, t, [(i, 2) for i in (1, 2)], True)
     first_pass(2)
+    second_pass(0)
     second_pass(1)
+    for k in range(CHUNKS):
+        sent(k)
+    sent_features()
+    exchanged(0, 0, ex_s)
+    exchanged(0, 1, ex_s)
     last_pass(0)
-    sent(0)
-    sent(1)
-    second_pass(2)
+    exchanged(1, 0, ex_s)
     last_pass(1)
-    sent(2)
-    sent_features()
-    for k in range(CHUNKS):
-        exchanged(0, k, ex_s)
-    exchanged(1, 0, ex_s)
     exchanged(1, 1, ex_s)
-    for k in range(CHUNKS - 1):
-        for sub in SUBS[k]:
-            put_out(sub)
-    last_pass(2)
-    exchanged(1, 2, ex_s)
-    put_out(SUBS[2][0])
+    for sub in range(GROUPS):
+        put_out(sub)
 
 
 def copy_out(src, dst, buf, load, store):
@@ -529,8 +544,8 @@
             dma((3, 2)),
             dma((7,)),
             dma((7,)),
-            dma((2, CHUNKS)),
-            dma((2, CHUNKS)),
+            dma((2, len(PASSES))),
+            dma((2, len(PASSES))),
             dma((GROUPS,)),
             dma((GROUPS,)),
             dma((GROUPS,)),

time: 97.5 us -> 94.6 us (0.970)
  Pallas kernels: 97.2 us -> 94.2 us
    pallas_call x1, Pallas kernels: 94.8 us -> 91.8 us  [body(): pl.pallas_call(kernel, out_shape=jax.ShapeDtypeStruct((TOK, 2 * HALF), f3...]
where the time goes in v4:
time: 94.6 us; the launch traced here: 94.4 us
  Pallas kernels  94.2 us (100%)
    pallas_call x1, Pallas kernels, body(): pl.pallas_call(kernel, out_shape=jax.ShapeDtypeStruct((TOK, 2 * HALF), f3...  91.8 us
    pallas_call x1, Pallas kernels, body(): pl.pallas_call(copy_out, out_shape=jax.ShapeDtypeStruct((TOK, 2 * HALF),...  2.39 us

profile of v4, /device:TPU:1, one launch (start us, length us, event | category | flops | bytes accessed | tf_op | source)
XLA Modules:
  0.0 94.4 jit_solution(18430157019196406667)
XLA Ops:
  0.0 91.8 %shard_map.55.src = f32[512,1024]{1,0:T(8,128)} custom-call(bf16[512,1024]{1,0:T(8,128)(2,1)} %tok_hbm.1, bf16[3,128,1024]{2,1,0:T(8,128)(2,1)} %w_hbm.1, f32[3,1024]{1,0:T(4,128)} %bias.1, f32[3,1024]{1,0:T(4,128)} %rec.1, f32[1,1024]{1,0:T(1,128)} %bitcast.1), custom_call_target="tpu_custom_call" | custom-call | flops 12884901888 | bytes 8388608 | tf_op jit(solution)/shard_map/pallas_call | solution.py:521
  91.9 2.4 %shard_map.56 = f32[512,1024]{1,0:T(8,128)} custom-call(f32[512,1024]{1,0:T(8,128)} %shard_map.55.src), custom_call_target="tpu_custom_call" | custom-call | tf_op jit(solution)/shard_map/pallas_call | solution.py:560

commit v5 on v4

--- a/solution.py
+++ b/solution.py
@@ -59,8 +59,8 @@
 
 
 def kernel(
-    tok_hbm, w_hbm, bias, rec, init, out,
-    X, W0, W1, W2, PRE, AB1, AB2, OUTB, SEGT, MID, SUM, SLOT,
+    tok_hbm, w_hbm, bias_hbm, rec_hbm, init_hbm, out,
+    X, W0, W1, W2, bias, rec, init, PRE, AB1, AB2, OUTB, SEGT, MID, SUM, SLOT,
     local_sem, sib_s, sib_r, w_s, p1_r, p2_r, t_s, t_r, ts_s, ts_r, ex_s, ex_r, o_l, o_s, o_r,
 ):
     W = (W0, W1, W2)
@@ -113,6 +113,10 @@
     def tcols(xx):
         return pl.ds(pl.multiple_of(lax.rem(xx, RING) * FEAT, FEAT), FEAT)
 
+    barrier = pltpu.get_barrier_semaphore()
+
+    for d in (right, left, up, down, xr, xl, sib):
+        pl.semaphore_signal(barrier, inc=1, device_id=d, device_id_type=MESH)
     mine = pl.ds(pl.multiple_of(q * 256 + c * 128, 128), 128)
     own_tok = pltpu.make_async_copy(tok_hbm, X.at[trows(c), tcols(x)], local_sem.at[CHUNKS])
     for k in range(CHUNKS):
@@ -123,11 +127,13 @@
                 local_sem.at[k],
             ).start()
     own_tok.start()
-
-    barrier = pltpu.get_barrier_semaphore()
-
-    for d in (right, left, up, down, xr, xl, sib):
-        pl.semaphore_signal(barrier, inc=1, device_id=d, device_id_type=MESH)
+    small = [
+        pltpu.make_async_copy(src, dst, local_sem.at[CHUNKS + 1 + n])
+        for n, (src, dst) in enumerate(((bias_hbm, bias), (rec_hbm, rec), (init_hbm, init)))
+    ]
+    for cp in small:
+        cp.start()
+
     pl.semaphore_wait(barrier, 7)
 
     def own_rows(k):
@@ -414,6 +420,8 @@
     send2(0, 2)
     send2b(0, 2)
     features_first()
+    for cp in small:
+        cp.wait()
     pass_on(0, 0)
     pass_on(0, 3)
     own_rows(1)
@@ -495,21 +503,14 @@
         put_out(sub)
 
 
-def copy_out(src, dst, buf, load, store):
+def copy_out(src, dst, store):
     rows = TOK // 8
-    ins = [
-        pltpu.make_async_copy(src.at[pl.ds(i * rows, rows)], buf.at[pl.ds(i * rows, rows)], load.at[i])
+    outs = [
+        pltpu.make_async_copy(src.at[pl.ds(i * rows, rows)], dst.at[pl.ds(i * rows, rows)], store.at[i])
         for i in range(8)
     ]
-    outs = [
-        pltpu.make_async_copy(buf.at[pl.ds(i * rows, rows)], dst.at[pl.ds(i * rows, rows)], store.at[i])
-        for i in range(8)
-    ]
-    for cp in ins:
+    for cp in outs:
         cp.start()
-    for cp, nxt in zip(ins, outs):
-        cp.wait()
-        nxt.start()
     for cp in outs:
         cp.wait()
 
@@ -517,15 +518,20 @@
 def body(tokens, weights, gate_bias, recurrent, initial_state):
     dma = pltpu.SemaphoreType.DMA
     f32, bf16 = jnp.float32, jnp.bfloat16
-    vmem, hbm = pl.BlockSpec(memory_space=pltpu.VMEM), pl.BlockSpec(memory_space=pl.ANY)
+    hbm = pl.BlockSpec(memory_space=pl.ANY)
+    args = (tokens, weights, gate_bias, recurrent, initial_state[None, :])
+    args = [pltpu.with_memory_space_constraint(a, pltpu.HBM) for a in args]
     states = pl.pallas_call(
         kernel,
         out_shape=jax.ShapeDtypeStruct((TOK, 2 * HALF), f32),
-        in_specs=[hbm, hbm, vmem, vmem, vmem],
+        in_specs=[hbm] * 5,
         out_specs=hbm,
         scratch_shapes=[
             pltpu.VMEM((ROWS, DEPTH), bf16),
             *[pltpu.VMEM((DEPTH, 3 * w), bf16) for w in WIDTHS],
+            pltpu.VMEM((3, 2 * HALF), f32),
+            pltpu.VMEM((3, 2 * HALF), f32),
+            pltpu.VMEM((1, 2 * HALF), f32),
             pltpu.VMEM((GROUPS, 3, 2, TOK, CH), f32),
             pltpu.VMEM((GROUPS, 2, 2, TOK, CH), f32),
             pltpu.VMEM((GROUPS, 2, 2, TOK, CH), f32),
@@ -534,7 +540,7 @@
             pltpu.VMEM((2, GROUPS, SEGS, CH), f32),
             pltpu.VMEM((2, GROUPS, SEGS, CH), f32),
             pltpu.VMEM((2, CHIPS, GROUPS, SEGS, CH), f32),
-            dma((CHUNKS + 1,)),
+            dma((CHUNKS + 4,)),
             dma((CHUNKS,)),
             dma((CHUNKS,)),
             dma((CHUNKS,)),
@@ -551,19 +557,19 @@
             dma((GROUPS,)),
         ],
         compiler_params=pltpu.CompilerParams(
-            collective_id=0, has_side_effects=True, vmem_limit_bytes=56 * 2**20
+            collective_id=0, has_side_effects=True, vmem_limit_bytes=47 * 2**20
         ),
         cost_estimate=pl.CostEstimate(
             flops=2 * ROWS * DEPTH * 3 * HALF, bytes_accessed=8 * 2**20, transcendentals=0
         ),
-    )(tokens, weights, gate_bias, recurrent, initial_state[None, :])
+    )(*args)
     return pl.pallas_call(
         copy_out,
         out_shape=jax.ShapeDtypeStruct((TOK, 2 * HALF), f32),
-        in_specs=[hbm],
+        in_specs=[pl.BlockSpec(memory_space=pltpu.VMEM)],
         out_specs=hbm,
-        scratch_shapes=[pltpu.VMEM((TOK, 2 * HALF), f32), dma((8,)), dma((8,))],
-        compiler_params=pltpu.CompilerParams(vmem_limit_bytes=56 * 2**20),
+        scratch_shapes=[dma((8,))],
+        compiler_params=pltpu.CompilerParams(vmem_limit_bytes=16 * 2**20),
     )(states)
 
 

time: 94.6 us -> 92.6 us (0.979)
  Pallas kernels: 94.2 us -> 92.4 us
    pallas_call x1, Pallas kernels: 2.39 us -> 1.38 us  [body(): pl.pallas_call(copy_out, out_shape=jax.ShapeDtypeStruct((TOK, 2 * HALF),...]
where the time goes in v5:
time: 92.6 us; the launch traced here: 92.5 us
  Pallas kernels  92.4 us (100%)
    pallas_call x1, Pallas kernels, body(): pl.pallas_call(kernel, out_shape=jax.ShapeDtypeStruct((TOK, 2 * HALF), f3...  91 us

profile of v5, /device:TPU:1, one launch (start us, length us, event | category | flops | bytes accessed | tf_op | source)
XLA Modules:
  0.0 92.5 jit_solution(5319303449170158842)
XLA Ops:
  0.0 91.0 %shard_map.55.src = f32[512,1024]{1,0:T(8,128)S(1)} custom-call(bf16[512,1024]{1,0:T(8,128)(2,1)} %tok_hbm.1, bf16[3,128,1024]{2,1,0:T(8,128)(2,1)} %w_hbm.1, f32[3,1024]{1,0:T(4,128)} %bias_hbm.1, f32[3,1024]{1,0:T(4,128)} %rec_hbm.1, f32[1,1024]{1,0:T(1,128)} %bitcast.1), custom_call_target="tpu_custom_call" | custom-call | flops 12884901888 | bytes 8388608 | tf_op jit(solution)/shard_map/pallas_call | solution.py:524
  91.0 1.4 %shard_map.56 = f32[512,1024]{1,0:T(8,128)} custom-call(f32[512,1024]{1,0:T(8,128)S(1)} %shard_map.55.src), custom_call_target="tpu_custom_call" | custom-call | tf_op jit(solution)/shard_map/pallas_call | solution.py:566

commit v6 on v5

--- a/solution.py
+++ b/solution.py
@@ -360,18 +360,23 @@
         publish(1, sub, [(A, B) for _, A, B in carry])
 
     def pass3(sub):
-        def group(t, hs):
-            for o in range(UN):
-                j = t * UN + o
-                v = vreg(j)
-                hs = [AB2[sub, 0, m, v, :] * hs[m] + AB2[sub, 1, m, v, :] for m in range(2)]
-                for m in range(2):
-                    OUTB[sub, pl.ds(m * TOK + j, SEGS, stride=SEG), :] = hs[m]
-            return hs
-
-        lax.fori_loop(0, SEG // UN, group, incoming(1, sub))
+        incoming(1, sub)
         here = out.at[:, lanes(c, sub)]
+
+        def tokens_of(m):
+            def group(t, h):
+                for o in range(UN):
+                    j = t * UN + o
+                    v = vreg(j)
+                    h = AB2[sub, 0, m, v, :] * h + AB2[sub, 1, m, v, :]
+                    OUTB[sub, pl.ds(m * TOK + j, SEGS, stride=SEG), :] = h
+                return h
+
+            lax.fori_loop(0, SEG // UN, group, SEGT[1, sub, m, 2])
+
+        tokens_of(1 - c)
         rcopy(OUTB.at[sub, trows(1 - c)], here, o_s.at[sub], o_r.at[sub], sib).start()
+        tokens_of(c)
         pltpu.make_async_copy(OUTB.at[sub, trows(c)], here, o_l.at[sub]).start()
 
     def put_out(sub):

time: 92.6 us -> 92.4 us (level)
  no operation moved by 1% of the time
where the time goes in v6:
time: 92.4 us; the launch traced here: 92.3 us
  Pallas kernels  92.1 us (100%)
    pallas_call x1, Pallas kernels, body(): pl.pallas_call(kernel, out_shape=jax.ShapeDtypeStruct((TOK, 2 * HALF), f3...  90.7 us

profile of v6, /device:TPU:1, one launch (start us, length us, event | category | flops | bytes accessed | tf_op | source)
XLA Modules:
  0.0 92.3 jit_solution(11818811378045318020)
XLA Ops:
  0.0 90.7 %shard_map.55.src = f32[512,1024]{1,0:T(8,128)S(1)} custom-call(bf16[512,1024]{1,0:T(8,128)(2,1)} %tok_hbm.1, bf16[3,128,1024]{2,1,0:T(8,128)(2,1)} %w_hbm.1, f32[3,1024]{1,0:T(4,128)} %bias_hbm.1, f32[3,1024]{1,0:T(4,128)} %rec_hbm.1, f32[1,1024]{1,0:T(1,128)} %bitcast.1), custom_call_target="tpu_custom_call" | custom-call | flops 12884901888 | bytes 8388608 | tf_op jit(solution)/shard_map/pallas_call | solution.py:529
  90.7 1.4 %shard_map.56 = f32[512,1024]{1,0:T(8,128)} custom-call(f32[512,1024]{1,0:T(8,128)S(1)} %shard_map.55.src), custom_call_target="tpu_custom_call" | custom-call | tf_op jit(solution)/shard_map/pallas_call | solution.py:571
